TPU v7x, 32 devices: a whole 2x2x4 slice. The times are simulated.
32 devices in a mesh: row: 2 (over x), col: 16 (over z, y, core).
Axes of the slice: x: 2, y: 2, z: 4, core: 2. Of those that a mesh axis runs over, the one named last changes fastest.
Arguments:
- landmarks: bfloat16 [8192, 768], P(('row', 'col')), may hold values from -1 to 1
- jitter: bfloat16 [8192], P('col'), may hold values from 0.049804688 to 0.5
Outputs:
- panel: float32 [8192, 512], P('row')
- schur: float32 [8192, 8192], P('row', 'col')
All inputs are finite; a program needn't handle non-finite values.
Results may differ from a plain program's by a relative error of at most 0.0003.
Values may be sent and summed in bfloat16 or wider, within the bound.
A program may use at most 128 MiB of HBM per device.

v0:
```python
import functools

import jax
import jax.numpy as jnp
from jax import lax
from jax.experimental import pallas as pl
from jax.experimental.pallas import tpu as pltpu
from jax.sharding import PartitionSpec as P

kernel_rate = 1.5
MESH = pl.DeviceIdType.MESH
BLOCK = 128
STRIP = 8
Z_PARTS = 4
CORES = 2


def dot_t(left, right, **kwargs):
    return lax.dot_general(
        left, right, (((1,), (1,)), ((), ())), preferred_element_type=jnp.float32, **kwargs
    )


def dot_n(left, right):
    return lax.dot_general(
        left,
        right,
        (((1,), (0,)), ((), ())),
        precision=lax.Precision.HIGHEST,
        preferred_element_type=jnp.float32,
    )


def split(values):
    high = values.astype(jnp.bfloat16)
    low = (values - high.astype(jnp.float32)).astype(jnp.bfloat16)
    return high, low


def dot3_t(left, right):
    (lh, ll), (rh, rl) = left, right
    return dot_t(lh, rh) + (dot_t(lh, rl) + dot_t(ll, rh))


def squares_of(points):
    values = points.astype(jnp.float32)
    return jnp.sum(values * values, axis=1, keepdims=True)


def as_row(column):
    wide = jnp.broadcast_to(column, (column.shape[0], BLOCK))
    return wide.T[0:1, :]


def gram_of(left, right, left_sq, right_row):
    cross = dot_t(left, right)
    return jnp.exp(-kernel_rate * (left_sq + right_row - 2.0 * cross))


def on_diagonal(values, offset, jit_row):
    rows = lax.broadcasted_iota(jnp.int32, values.shape, 0)
    cols = lax.broadcasted_iota(jnp.int32, values.shape, 1)
    return values + jnp.where(rows - cols == offset, jit_row, 0.0)


def invert_block(block):
    n = BLOCK // STRIP
    sub = lax.broadcasted_iota(jnp.int32, (STRIP, BLOCK), 0)
    lane = lax.broadcasted_iota(jnp.int32, (STRIP, BLOCK), 1)
    a = [block[STRIP * i : STRIP * (i + 1), :] for i in range(n)]
    y = [jnp.where(lane == sub + STRIP * i, 1.0, 0.0).astype(jnp.float32) for i in range(n)]
    shape = (STRIP, BLOCK)
    for s in range(n):
        def column(strip, j):
            return jnp.broadcast_to(strip[:, STRIP * s + j : STRIP * s + j + 1], shape)

        r, q = a[s], y[s]
        b = [column(r, j) for j in range(STRIP)]
        rows, qrows, brows, pivots = [], [], [], []
        scale = jnp.zeros(shape, jnp.float32)
        for j in range(STRIP):
            take = lambda v: jnp.broadcast_to(v[j : j + 1, :], shape)
            inverse = 1.0 / take(b[j])
            scale = jnp.where(sub == j, inverse, scale)
            f = jnp.where(sub > j, b[j], 0.0) * inverse
            pivots.append(inverse)
            brow = {jj: take(b[jj]) for jj in range(j + 1, STRIP)}
            brows.append(brow)
            for jj in range(j + 1, STRIP):
                b[jj] = b[jj] - f * brow[jj]
            rows.append(take(r))
            qrows.append(take(q))
            r = r - f * rows[-1]
            q = q - f * qrows[-1]
        y[s] = q * lax.sqrt(scale)
        for t in range(s + 1, n):
            c = [column(a[t], j) for j in range(STRIP)]
            at, yt = a[t], y[t]
            for j in range(STRIP):
                f = c[j] * pivots[j]
                for jj in range(j + 1, STRIP):
                    c[jj] = c[jj] - f * brows[j][jj]
                at = at - f * rows[j]
                yt = yt - f * qrows[j]
            a[t], y[t] = at, yt
    return jnp.concatenate(y, axis=0)


def factor_inverse(points, jit_row, s_ref, y_ref):
    tile = points.shape[0]
    sq = squares_of(points)
    s_ref[...] = on_diagonal(gram_of(points, points, sq, as_row(sq)), 0, jit_row)
    rows = lax.broadcasted_iota(jnp.int32, (tile, tile), 0)
    cols = lax.broadcasted_iota(jnp.int32, (tile, tile), 1)
    y_ref[...] = jnp.where(rows == cols, 1.0, 0.0).astype(jnp.float32)

    def step(block, carry):
        here = pl.ds(pl.multiple_of(block * BLOCK, BLOCK), BLOCK)
        v = invert_block(s_ref[here, here])
        u = dot_n(v, s_ref[here, :])
        x = dot_n(v, y_ref[here, :])
        below = dot_t(s_ref[:, here], v, precision=lax.Precision.HIGHEST)
        ids = lax.broadcasted_iota(jnp.int32, below.shape, 0)
        below = jnp.where(ids >= (block + 1) * BLOCK, below, 0.0)
        s_ref[...] -= dot_n(below, u)
        y_ref[...] -= dot_n(below, x)
        y_ref[here, :] = x
        return carry

    lax.fori_loop(0, tile // BLOCK, step, 0)


def factor_kernel(points_ref, jit_ref, high_ref, low_ref, s_ref, y_ref):
    factor_inverse(points_ref[...], jit_ref[0:1, :], s_ref, y_ref)
    high_ref[...], low_ref[...] = split(y_ref[...])


def factor_call(points, jit):
    tile = points.shape[0]
    out = jax.ShapeDtypeStruct((tile, tile), jnp.bfloat16)
    return pl.pallas_call(
        factor_kernel,
        out_shape=(out, out),
        scratch_shapes=[pltpu.VMEM((tile, tile), jnp.float32)] * 2,
        compiler_params=pltpu.CompilerParams(vmem_limit_bytes=32 << 20),
        name="factor",
    )(points, jit)


def schur_kernel(per_row, rows_ref, cols_ref, first_ref, xh_ref, xl_ref, jit_ref, first_jit_ref,
                 panel_ref, schur_ref, col_row_ref, first_row_ref, ph_ref, pl_ref):
    step = pl.program_id(0)
    row_index = lax.axis_index("row")
    col_index = lax.axis_index("col")
    bm = rows_ref.shape[0]
    tile = cols_ref.shape[0]
    row_start = (row_index * pl.num_programs(0) + step) * bm
    col_start = col_index * tile
    inverse = (xh_ref[...], xl_ref[...])

    @pl.when(step == 0)
    def _():
        col_sq = squares_of(cols_ref[...])
        col_row_ref[...] = as_row(col_sq)
        first_row_ref[...] = as_row(squares_of(first_ref[...]))
        part = gram_of(cols_ref[...], first_ref[...], col_sq, first_row_ref[...])
        part = on_diagonal(part, -col_start, first_jit_ref[0:1, :])
        ph_ref[...], pl_ref[...] = split(dot3_t(split(part), inverse))

    points = rows_ref[...]
    sq = squares_of(points)
    part = gram_of(points, first_ref[...], sq, first_row_ref[...])
    part = on_diagonal(part, -row_start, first_jit_ref[0:1, :])
    panel = dot3_t(split(part), inverse)
    panel_ref[...] = panel
    block = gram_of(points, cols_ref[...], sq, col_row_ref[...])
    block = on_diagonal(block, col_start - row_start, jit_ref[0:1, :])
    schur_ref[...] = block - dot3_t(split(panel), (ph_ref[...], pl_ref[...]))


def schur_call(per_row, row_pts, col_pts, first_pts, xh, xl, jit, first_jit):
    rowb, width = row_pts.shape
    tile = col_pts.shape[0]
    bm = min(512, rowb)
    whole = lambda shape: pl.BlockSpec(shape, lambda i: (0, 0))
    out = jax.ShapeDtypeStruct((rowb, tile), jnp.float32)
    return pl.pallas_call(
        functools.partial(schur_kernel, per_row),
        grid=(rowb // bm,),
        in_specs=[
            pl.BlockSpec((bm, width), lambda i: (i, 0)),
            whole((tile, width)),
            whole((tile, width)),
            whole((tile, tile)),
            whole((tile, tile)),
            whole((8, tile)),
            whole((8, tile)),
        ],
        out_specs=[pl.BlockSpec((bm, tile), lambda i: (i, 0))] * 2,
        out_shape=(out, out),
        scratch_shapes=[
            pltpu.VMEM((1, tile), jnp.float32),
            pltpu.VMEM((1, tile), jnp.float32),
            pltpu.VMEM((tile, tile), jnp.bfloat16),
            pltpu.VMEM((tile, tile), jnp.bfloat16),
        ],
        compiler_params=pltpu.CompilerParams(vmem_limit_bytes=48 << 20),
        name="schur",
    )(row_pts, col_pts, first_pts, xh, xl, jit, first_jit)


def gather_kernel(rows, cols, own_ref, jit_ref, out_ref, col_ref, first_ref, first_jit_ref,
                  send_z, send_y, send_k, recv, send_x, recv_x, send_f, recv_f, send_fk,
                  recv_fk, send_j, recv_j, local):
    me_row = lax.axis_index("row")
    me = lax.axis_index("col")
    size = own_ref.shape[0]
    tile = col_ref.shape[0]
    spc = tile // size
    per_row = cols // rows
    y_parts = cols // (Z_PARTS * CORES)
    core = lax.rem(me, CORES)
    my_y = lax.rem(me // CORES, y_parts)
    my_z = me // (CORES * y_parts)
    sibling = me + 1 - 2 * core

    def index(z, y, k):
        return (z * y_parts + y) * CORES + k

    def z_peer(d):
        return lax.rem(my_z + d, Z_PARTS)

    def y_peer(d):
        return lax.rem(my_y + d, y_parts)

    def row_peer(d):
        return lax.rem(me_row + d, rows)

    shard = me_row * cols + me
    tile_of = shard // spc
    place = lax.rem(shard, spc)
    home = me // per_row

    def part(ref, i, count=1):
        return ref.at[pl.ds(pl.multiple_of(i * size, size), count * size)]

    def tell(row, col):
        pl.semaphore_signal(
            barrier, inc=1, device_id=(row, col), device_id_type=MESH
        )

    barrier = pltpu.get_barrier_semaphore()
    tell(me_row, sibling)
    for d in range(1, Z_PARTS):
        tell(me_row, index(z_peer(d), my_y, core))
    for d in range(1, y_parts):
        tell(me_row, index(my_z, y_peer(d), core))
    count = 1 + (Z_PARTS - 1) + (y_parts - 1)
    for d in range(1, rows):
        tell(row_peer(d), me)
    count += rows - 1
    for i in range(spc):
        source = me * spc + i
        source_row = source // cols

        @pl.when(source_row != me_row)
        def _():
            tell(source_row, lax.rem(source, cols))
    count += rows - 1

    @pl.when(me != 0)
    def _():
        tell(me_row, 0)

    @pl.when(me != 0)
    def _():
        pl.semaphore_wait(barrier, count)

    @pl.when(me == 0)
    def _():
        pl.semaphore_wait(barrier, count + cols - 1)

    def remote(src, dst, send, recv_sem, row, col):
        return pltpu.make_async_remote_copy(
            src_ref=src, dst_ref=dst, send_sem=send, recv_sem=recv_sem,
            device_id=(row, col), device_id_type=MESH,
        )

    def landed(dst, recv_sem):
        remote(dst, dst, send_j.at[0], recv_sem, me_row, sibling).wait_recv()

    own = part(out_ref, me)
    sends = []

    def go(*args):
        copy = remote(*args)
        copy.start()
        sends.append(copy)

    for d in range(1, Z_PARTS):
        go(own_ref, own, send_z.at[d], recv.at[me], me_row, index(z_peer(d), my_y, core))
    for d in range(1, y_parts):
        go(own_ref, own, send_y.at[0, d], recv.at[me], me_row, index(my_z, y_peer(d), core))
    go(own_ref, own, send_k.at[0, 0], recv.at[me], me_row, sibling)
    for d in range(1, rows):
        go(own_ref, part(col_ref, place), send_x.at[d], recv_x.at[place], row_peer(d), tile_of)

    @pl.when(me == 0)
    def _():
        for c in range(1, cols):
            remote(jit_ref, first_jit_ref, send_j.at[c], recv_j, me_row, c).start()
        copy = pltpu.make_async_copy(jit_ref, first_jit_ref, local.at[1])
        copy.start()
        copy.wait()

    mine = pltpu.make_async_copy(own_ref, own, local.at[0])
    mine.start()

    for i, dz in enumerate((1, Z_PARTS - 1, 2)):
        source = index(z_peer(dz), my_y, core)
        landed(part(out_ref, source), recv.at[source])
        for d in range(1, y_parts):
            go(part(out_ref, source), part(out_ref, source), send_y.at[dz, d], recv.at[source],
               me_row, index(my_z, y_peer(d), core))
        go(part(out_ref, source), part(out_ref, source), send_k.at[dz, 0], recv.at[source],
           me_row, sibling)
    mine.wait()
    for dz in (0, 1, Z_PARTS - 1, 2):
        for d in range(1, y_parts):
            source = index(z_peer(dz), y_peer(d), core)
            landed(part(out_ref, source), recv.at[source])
            go(part(out_ref, source), part(out_ref, source), send_k.at[dz, d], recv.at[source],
               me_row, sibling)
    for dz in range(Z_PARTS):
        for d in range(y_parts):
            source = index(z_peer(dz), y_peer(d), 1 - core)
            landed(part(out_ref, source), recv.at[source])

    half = tile // CORES

    def piece(ref, k):
        return ref.at[pl.ds(pl.multiple_of(k * half, half), half)]

    @pl.when(me_row == 0)
    def _():
        copy = pltpu.make_async_copy(out_ref.at[pl.ds(0, tile)], first_ref, local.at[2])
        copy.start()
        for d in range(1, rows):
            remote(piece(out_ref, core), piece(first_ref, core), send_f.at[d], recv_f,
                   d, me).start()
        copy.wait()
        for d in range(1, rows):
            remote(piece(out_ref, core), piece(first_ref, core), send_f.at[d], recv_f,
                   d, me).wait_send()

    @pl.when(me_row != 0)
    def _():
        landed(piece(first_ref, core), recv_f)
        copy = remote(piece(first_ref, core), piece(first_ref, core), send_fk, recv_fk,
                      me_row, sibling)
        copy.start()
        copy.wait_send()
        landed(piece(first_ref, 1 - core), recv_fk)

    @pl.when(home == me_row)
    def _():
        start = pl.multiple_of(lax.rem(me, per_row) * tile, tile)
        copy = pltpu.make_async_copy(out_ref.at[pl.ds(start, tile)], col_ref, local.at[3])
        copy.start()
        copy.wait()

    @pl.when(home != me_row)
    def _():
        for i in range(spc):
            landed(part(col_ref, i), recv_x.at[i])

    @pl.when(me == 0)
    def _():
        for c in range(1, cols):
            remote(jit_ref, first_jit_ref, send_j.at[c], recv_j, me_row, c).wait_send()

    @pl.when(me != 0)
    def _():
        landed(first_jit_ref, recv_j)

    for copy in sends:
        copy.wait_send()


def gather_call(rows, cols, landmarks, jit):
    size, width = landmarks.shape
    tile = jit.shape[1]
    y_parts = cols // (Z_PARTS * CORES)
    dma = pltpu.SemaphoreType.DMA
    return pl.pallas_call(
        functools.partial(gather_kernel, rows, cols),
        in_specs=[pl.BlockSpec(memory_space=pl.ANY)] * 2,
        out_specs=[pl.BlockSpec(memory_space=pl.ANY)] * 4,
        out_shape=(
            jax.ShapeDtypeStruct((cols * size, width), landmarks.dtype),
            jax.ShapeDtypeStruct((tile, width), landmarks.dtype),
            jax.ShapeDtypeStruct((tile, width), landmarks.dtype),
            jax.ShapeDtypeStruct(jit.shape, jit.dtype),
        ),
        scratch_shapes=[
            dma((Z_PARTS,)),
            dma((Z_PARTS, y_parts)),
            dma((Z_PARTS, y_parts)),
            dma((cols,)),
            dma((rows,)),
            dma((tile // size,)),
            dma((rows,)),
            dma,
            dma,
            dma,
            dma((cols,)),
            dma,
            dma((4,)),
        ],
        compiler_params=pltpu.CompilerParams(collective_id=0, has_side_effects=True),
        name="gather",
    )(landmarks, jit)


def local(landmarks, jitter):
    rows = lax.axis_size("row")
    cols = lax.axis_size("col")
    tile = jitter.shape[0]
    jit = jnp.broadcast_to(jitter.astype(jnp.float32)[None, :], (8, tile))
    row_pts, col_pts, first_pts, first_jit = gather_call(rows, cols, landmarks, jit)
    xh, xl = factor_call(first_pts, first_jit)
    return tuple(schur_call(cols // rows, row_pts, col_pts, first_pts, xh, xl, jit, first_jit))


def solution(mesh):
    in_specs = (P(("row", "col"), None), P("col"))
    out_specs = (P("row", None), P("row", "col"))
    return jax.shard_map(local, mesh=mesh, in_specs=in_specs, out_specs=out_specs, check_vma=False)
```

profile of v0, /device:TPU:9, one launch (start us, length us, event | category | flops | bytes accessed | tf_op | source)
XLA Modules:
  0.0 189.8 jit_solution(13627775441331269887)
XLA Ops:
  0.6 1.3 broadcast_in_dim.2.jit_ref
  1.9 125.9 %gather.1 = (bf16[4096,768]{1,0:T(8,128)(2,1)}, bf16[512,768]{1,0:T(8,128)(2,1)}, bf16[512,768]{1,0:T(8,128)(2,1)}, f32[8,512]{1,0:T(8,128)}) custom-call(bf16[256,768]{1,0:T(8,128)(2,1)} %own_ref.1, f32[8,512]{1,0:T(8,128)} %broadcast_in_dim.2.jit_ref), custom_call_target="tpu_custom_call" | custom-call | tf_op jit(solution)/shard_map/gather/pallas_call | solution.py:395
  127.8 0.0 copy-start
  127.8 1.1 copy-done
  128.9 0.0 copy-start.4
  128.9 0.7 copy-done.4
  129.7 28.2 %factor.1 = (bf16[512,512]{1,0:T(8,128)(2,1)S(1)}, bf16[512,512]{1,0:T(8,128)(2,1)S(1)}) custom-call(bf16[512,768]{1,0:T(8,128)(2,1)S(1)} %copy-done, f32[8,512]{1,0:T(8,128)S(1)} %copy-done.4), custom_call_target="tpu_custom_call" | custom-call | tf_op jit(solution)/shard_map/factor/pallas_call | solution.py:141
  157.9 0.0 copy-start.1
  157.9 1.1 copy-done.1
  159.0 0.0 copy-start.2
  159.0 1.1 copy-done.2
  160.2 0.0 copy-start.3
  160.2 0.7 copy-done.3
  160.9 0.0 copy-start.5
  160.9 0.7 copy-done.5
  161.6 28.2 %schur.1 = (f32[4096,512]{1,0:T(8,128)}, f32[4096,512]{1,0:T(8,128)}) custom-call(bf16[4096,768]{1,0:T(8,128)(2,1)} %get-tuple-element.8.rows_ref, bf16[512,768]{1,0:T(8,128)(2,1)S(1)} %copy-done.2, bf16[512,768]{1,0:T(8,128)(2,1)S(1)} %copy-done.1, bf16[512,512]{1,0:T(8,128)(2,1)S(1)} %get-tuple-element.12.xh_ref, ...), custom_call_target="tpu_custom_call" | custom-call | tf_op jit(solution)/shard_map/schur/pallas_call | solution.py:187
Async XLA Ops:
  127.8 1.1 copy-start
  128.9 0.7 copy-start.4
  157.9 1.1 copy-start.1
  159.0 1.1 copy-start.2
  160.2 0.7 copy-start.3
  160.9 0.7 copy-start.5
where the time goes:
time: 190 us
  Pallas kernels  182 us (96%)
  local copies, waits for them, and re-layouts  6.82 us (4%)
    pallas_call x1, Pallas kernels, gather_call(): pl.pallas_call(functools.partial(gather_kernel, rows, cols), in_specs=[pl...  126 us
    pallas_call x1, Pallas kernels, schur_call(): pl.pallas_call(functools.partial(schur_kernel, per_row), grid=(rowb // bm...  28.2 us
    pallas_call x1, Pallas kernels, factor_call(): pl.pallas_call(factor_kernel, out_shape=(out, out), scratch_shapes=[pltpu...  28.2 us
    unnamed x12, local copies, waits for them, and re-layouts  5.54 us

commit v1 on v0

--- a/solution.py
+++ b/solution.py
@@ -13,6 +13,7 @@
 STRIP = 8
 Z_PARTS = 4
 CORES = 2
+CHUNKS = 2
 
 
 def dot_t(left, right, **kwargs):
@@ -106,7 +107,7 @@
     return jnp.concatenate(y, axis=0)
 
 
-def factor_inverse(points, jit_row, s_ref, y_ref):
+def factor_inverse(points, jit_row, s_ref, y_ref, between):
     tile = points.shape[0]
     sq = squares_of(points)
     s_ref[...] = on_diagonal(gram_of(points, points, sq, as_row(sq)), 0, jit_row)
@@ -125,26 +126,10 @@
         s_ref[...] -= dot_n(below, u)
         y_ref[...] -= dot_n(below, x)
         y_ref[here, :] = x
+        between(block)
         return carry
 
     lax.fori_loop(0, tile // BLOCK, step, 0)
-
-
-def factor_kernel(points_ref, jit_ref, high_ref, low_ref, s_ref, y_ref):
-    factor_inverse(points_ref[...], jit_ref[0:1, :], s_ref, y_ref)
-    high_ref[...], low_ref[...] = split(y_ref[...])
-
-
-def factor_call(points, jit):
-    tile = points.shape[0]
-    out = jax.ShapeDtypeStruct((tile, tile), jnp.bfloat16)
-    return pl.pallas_call(
-        factor_kernel,
-        out_shape=(out, out),
-        scratch_shapes=[pltpu.VMEM((tile, tile), jnp.float32)] * 2,
-        compiler_params=pltpu.CompilerParams(vmem_limit_bytes=32 << 20),
-        name="factor",
-    )(points, jit)
 
 
 def schur_kernel(per_row, rows_ref, cols_ref, first_ref, xh_ref, xl_ref, jit_ref, first_jit_ref,
@@ -210,8 +195,8 @@
 
 
 def gather_kernel(rows, cols, own_ref, jit_ref, out_ref, col_ref, first_ref, first_jit_ref,
-                  send_z, send_y, send_k, recv, send_x, recv_x, send_f, recv_f, send_fk,
-                  recv_fk, send_j, recv_j, local):
+                  high_ref, low_ref, s_ref, y_ref, send_up, send_down, send_y, send_k, recv,
+                  send_x, recv_x, send_f, recv_f, send_fk, send_j, recv_j, local):
     me_row = lax.axis_index("row")
     me = lax.axis_index("col")
     size = own_ref.shape[0]
@@ -223,12 +208,10 @@
     my_y = lax.rem(me // CORES, y_parts)
     my_z = me // (CORES * y_parts)
     sibling = me + 1 - 2 * core
+    chunk = size // CHUNKS
 
     def index(z, y, k):
         return (z * y_parts + y) * CORES + k
-
-    def z_peer(d):
-        return lax.rem(my_z + d, Z_PARTS)
 
     def y_peer(d):
         return lax.rem(my_y + d, y_parts)
@@ -241,24 +224,30 @@
     place = lax.rem(shard, spc)
     home = me // per_row
 
-    def part(ref, i, count=1):
-        return ref.at[pl.ds(pl.multiple_of(i * size, size), count * size)]
+    def part(ref, i, h):
+        return ref.at[pl.ds(pl.multiple_of(i * size + h * chunk, chunk), chunk)]
+
+    def whole(ref, i):
+        return ref.at[pl.ds(pl.multiple_of(i * size, size), size)]
 
     def tell(row, col):
-        pl.semaphore_signal(
-            barrier, inc=1, device_id=(row, col), device_id_type=MESH
-        )
+        pl.semaphore_signal(barrier, inc=1, device_id=(row, col), device_id_type=MESH)
 
     barrier = pltpu.get_barrier_semaphore()
     tell(me_row, sibling)
-    for d in range(1, Z_PARTS):
-        tell(me_row, index(z_peer(d), my_y, core))
+
+    @pl.when(my_z > 0)
+    def _():
+        tell(me_row, index(my_z - 1, my_y, core))
+
+    @pl.when(my_z < Z_PARTS - 1)
+    def _():
+        tell(me_row, index(my_z + 1, my_y, core))
+
     for d in range(1, y_parts):
         tell(me_row, index(my_z, y_peer(d), core))
-    count = 1 + (Z_PARTS - 1) + (y_parts - 1)
     for d in range(1, rows):
         tell(row_peer(d), me)
-    count += rows - 1
     for i in range(spc):
         source = me * spc + i
         source_row = source // cols
@@ -266,19 +255,25 @@
         @pl.when(source_row != me_row)
         def _():
             tell(source_row, lax.rem(source, cols))
-    count += rows - 1
 
     @pl.when(me != 0)
     def _():
         tell(me_row, 0)
 
-    @pl.when(me != 0)
-    def _():
-        pl.semaphore_wait(barrier, count)
+    inner = 1 + 2 + (y_parts - 1) + 2 * (rows - 1)
+    ends = (Z_PARTS - 1) * CORES * y_parts
 
     @pl.when(me == 0)
     def _():
-        pl.semaphore_wait(barrier, count + cols - 1)
+        pl.semaphore_wait(barrier, inner - 1 + cols - 1)
+
+    @pl.when((me != 0) & ((my_z == 0) | (me >= ends)))
+    def _():
+        pl.semaphore_wait(barrier, inner - 1)
+
+    @pl.when((my_z > 0) & (me < ends))
+    def _():
+        pl.semaphore_wait(barrier, inner)
 
     def remote(src, dst, send, recv_sem, row, col):
         return pltpu.make_async_remote_copy(
@@ -289,78 +284,175 @@
     def landed(dst, recv_sem):
         remote(dst, dst, send_j.at[0], recv_sem, me_row, sibling).wait_recv()
 
-    own = part(out_ref, me)
-    sends = []
-
-    def go(*args):
-        copy = remote(*args)
+    def up(src, z, i, h):
+        return remote(src, part(out_ref, i, h), send_up.at[z, h], recv.at[i, h],
+                      me_row, index(my_z + 1, my_y, core))
+
+    def down(src, z, i, h):
+        return remote(src, part(out_ref, i, h), send_down.at[z, h], recv.at[i, h],
+                      me_row, index(my_z - 1, my_y, core))
+
+    def aside(src, z, d, i, h):
+        return remote(src, part(out_ref, i, h), send_y.at[z, d, h], recv.at[i, h],
+                      me_row, index(my_z, y_peer(d), core))
+
+    def across(src, z, y, h):
+        i = index(z, y, core)
+        return remote(src, part(out_ref, i, h), send_k.at[z, y, h], recv.at[i, h],
+                      me_row, sibling)
+
+    def walk(act, wait):
+        def spread(source, z, h, upward, downward):
+            i = index(z, my_y, core)
+            src = part(own_ref, 0, h) if source is own_ref else part(out_ref, i, h)
+            if wait:
+                landed(part(out_ref, i, h), recv.at[i, h])
+            if upward:
+                @pl.when(my_z < Z_PARTS - 1)
+                def _():
+                    act(up(src, z, i, h))
+            if downward:
+                @pl.when(my_z > 0)
+                def _():
+                    act(down(src, z, i, h))
+            for d in range(1, y_parts):
+                act(aside(src, z, d, i, h))
+            act(across(src, z, my_y, h))
+
+        for d in range(1, Z_PARTS):
+            for h in range(CHUNKS):
+                @pl.when(my_z >= d)
+                def _():
+                    spread(out_ref, my_z - d, h, True, False)
+
+                @pl.when(my_z + d < Z_PARTS)
+                def _():
+                    spread(out_ref, my_z + d, h, False, True)
+
+    def own_copies(act):
+        for h in range(CHUNKS):
+            src = part(own_ref, 0, h)
+
+            @pl.when(my_z < Z_PARTS - 1)
+            def _():
+                act(up(src, my_z, me, h))
+
+            @pl.when(my_z > 0)
+            def _():
+                act(down(src, my_z, me, h))
+
+            for d in range(1, y_parts):
+                act(aside(src, my_z, d, me, h))
+            act(across(src, my_z, my_y, h))
+
+    def to_columns(d):
+        return remote(own_ref, whole(col_ref, place), send_x.at[d], recv_x.at[place],
+                      row_peer(d), tile_of)
+
+    def jit_copy(c):
+        return remote(jit_ref, first_jit_ref, send_j.at[c], recv_j, me_row, c)
+
+    def begin(copy):
         copy.start()
-        sends.append(copy)
-
-    for d in range(1, Z_PARTS):
-        go(own_ref, own, send_z.at[d], recv.at[me], me_row, index(z_peer(d), my_y, core))
-    for d in range(1, y_parts):
-        go(own_ref, own, send_y.at[0, d], recv.at[me], me_row, index(my_z, y_peer(d), core))
-    go(own_ref, own, send_k.at[0, 0], recv.at[me], me_row, sibling)
-    for d in range(1, rows):
-        go(own_ref, part(col_ref, place), send_x.at[d], recv_x.at[place], row_peer(d), tile_of)
+
+    def finish(copy):
+        copy.wait_send()
+
+    own_copies(begin)
+    mine = pltpu.make_async_copy(own_ref, whole(out_ref, me), local.at[0])
+    mine.start()
 
     @pl.when(me == 0)
     def _():
         for c in range(1, cols):
-            remote(jit_ref, first_jit_ref, send_j.at[c], recv_j, me_row, c).start()
+            jit_copy(c).start()
         copy = pltpu.make_async_copy(jit_ref, first_jit_ref, local.at[1])
         copy.start()
         copy.wait()
 
-    mine = pltpu.make_async_copy(own_ref, own, local.at[0])
-    mine.start()
-
-    for i, dz in enumerate((1, Z_PARTS - 1, 2)):
-        source = index(z_peer(dz), my_y, core)
-        landed(part(out_ref, source), recv.at[source])
-        for d in range(1, y_parts):
-            go(part(out_ref, source), part(out_ref, source), send_y.at[dz, d], recv.at[source],
-               me_row, index(my_z, y_peer(d), core))
-        go(part(out_ref, source), part(out_ref, source), send_k.at[dz, 0], recv.at[source],
-           me_row, sibling)
+    walk(begin, True)
     mine.wait()
-    for dz in (0, 1, Z_PARTS - 1, 2):
-        for d in range(1, y_parts):
-            source = index(z_peer(dz), y_peer(d), core)
-            landed(part(out_ref, source), recv.at[source])
-            go(part(out_ref, source), part(out_ref, source), send_k.at[dz, d], recv.at[source],
-               me_row, sibling)
-    for dz in range(Z_PARTS):
-        for d in range(y_parts):
-            source = index(z_peer(dz), y_peer(d), 1 - core)
-            landed(part(out_ref, source), recv.at[source])
-
-    half = tile // CORES
-
-    def piece(ref, k):
-        return ref.at[pl.ds(pl.multiple_of(k * half, half), half)]
+
+    def first_copy(d, s, h):
+        return remote(part(out_ref, s, h), part(first_ref, s, h), send_f.at[d, s, h],
+                      recv_f.at[s, h], d, me)
+
+    def first_across(s, h):
+        return remote(part(first_ref, s, h), part(first_ref, s, h), send_fk.at[s, h],
+                      recv_f.at[s, h], me_row, sibling)
+
+    ahead = spc // CORES
+    for y in range(ahead):
+        s = index(0, y, core)
+        for h in range(CHUNKS):
+            @pl.when(my_y != y)
+            def _():
+                landed(part(out_ref, s, h), recv.at[s, h])
+                across(part(out_ref, s, h), 0, y, h).start()
+
+            @pl.when(me_row == 0)
+            def _():
+                for d in range(1, rows):
+                    first_copy(d, s, h).start()
+    for y in range(ahead):
+        s = index(0, y, core)
+        for h in range(CHUNKS):
+            @pl.when(me_row != 0)
+            def _():
+                landed(part(first_ref, s, h), recv_f.at[s, h])
+                first_across(s, h).start()
+
+    for d in range(1, rows):
+        to_columns(d).start()
+
+    for y in range(ahead):
+        s = index(0, y, 1 - core)
+        for h in range(CHUNKS):
+            landed(part(out_ref, s, h), recv.at[s, h])
+
+            @pl.when(me_row != 0)
+            def _():
+                landed(part(first_ref, s, h), recv_f.at[s, h])
 
     @pl.when(me_row == 0)
     def _():
         copy = pltpu.make_async_copy(out_ref.at[pl.ds(0, tile)], first_ref, local.at[2])
         copy.start()
-        for d in range(1, rows):
-            remote(piece(out_ref, core), piece(first_ref, core), send_f.at[d], recv_f,
-                   d, me).start()
         copy.wait()
-        for d in range(1, rows):
-            remote(piece(out_ref, core), piece(first_ref, core), send_f.at[d], recv_f,
-                   d, me).wait_send()
-
-    @pl.when(me_row != 0)
-    def _():
-        landed(piece(first_ref, core), recv_f)
-        copy = remote(piece(first_ref, core), piece(first_ref, core), send_fk, recv_fk,
-                      me_row, sibling)
-        copy.start()
-        copy.wait_send()
-        landed(piece(first_ref, 1 - core), recv_fk)
+
+    @pl.when(me != 0)
+    def _():
+        landed(first_jit_ref, recv_j)
+
+    def pass_on(z):
+        for d in range(1, y_parts):
+            y = y_peer(d)
+            i = index(z, y, core)
+
+            @pl.when(i >= spc)
+            def _():
+                for h in range(CHUNKS):
+                    landed(part(out_ref, i, h), recv.at[i, h])
+                    across(part(out_ref, i, h), z, y, h).start()
+
+    blocks = tile // BLOCK
+
+    def between(block):
+        @pl.when(block < Z_PARTS)
+        def _():
+            pass_on(block)
+
+    factor_inverse(first_ref[...], first_jit_ref[0:1, :], s_ref, y_ref, between)
+    high_ref[...], low_ref[...] = split(y_ref[...])
+    for z in range(blocks, Z_PARTS):
+        pass_on(z)
+
+    for z in range(Z_PARTS):
+        for y in range(y_parts):
+            if index(z, y, 0) >= spc:
+                i = index(z, y, 1 - core)
+                for h in range(CHUNKS):
+                    landed(part(out_ref, i, h), recv.at[i, h])
 
     @pl.when(home == me_row)
     def _():
@@ -372,52 +464,75 @@
     @pl.when(home != me_row)
     def _():
         for i in range(spc):
-            landed(part(col_ref, i), recv_x.at[i])
+            landed(whole(col_ref, i), recv_x.at[i])
+
+    own_copies(finish)
+    walk(finish, False)
+    for z in range(Z_PARTS):
+        for d in range(1, y_parts):
+            for h in range(CHUNKS):
+                y = y_peer(d)
+                finish(across(part(out_ref, index(z, y, core), h), z, y, h))
+    for d in range(1, rows):
+        finish(to_columns(d))
+    for y in range(ahead):
+        s = index(0, y, core)
+        for h in range(CHUNKS):
+            @pl.when(me_row == 0)
+            def _():
+                for d in range(1, rows):
+                    finish(first_copy(d, s, h))
+
+            @pl.when(me_row != 0)
+            def _():
+                finish(first_across(s, h))
 
     @pl.when(me == 0)
     def _():
         for c in range(1, cols):
-            remote(jit_ref, first_jit_ref, send_j.at[c], recv_j, me_row, c).wait_send()
-
-    @pl.when(me != 0)
-    def _():
-        landed(first_jit_ref, recv_j)
-
-    for copy in sends:
-        copy.wait_send()
+            finish(jit_copy(c))
 
 
 def gather_call(rows, cols, landmarks, jit):
     size, width = landmarks.shape
     tile = jit.shape[1]
+    spc = tile // size
     y_parts = cols // (Z_PARTS * CORES)
     dma = pltpu.SemaphoreType.DMA
+    vmem = pl.BlockSpec(memory_space=pltpu.VMEM)
+    hbm = pl.BlockSpec(memory_space=pl.ANY)
     return pl.pallas_call(
         functools.partial(gather_kernel, rows, cols),
-        in_specs=[pl.BlockSpec(memory_space=pl.ANY)] * 2,
-        out_specs=[pl.BlockSpec(memory_space=pl.ANY)] * 4,
+        in_specs=[hbm, vmem],
+        out_specs=[hbm, hbm, vmem, vmem, vmem, vmem],
         out_shape=(
             jax.ShapeDtypeStruct((cols * size, width), landmarks.dtype),
             jax.ShapeDtypeStruct((tile, width), landmarks.dtype),
             jax.ShapeDtypeStruct((tile, width), landmarks.dtype),
             jax.ShapeDtypeStruct(jit.shape, jit.dtype),
+            jax.ShapeDtypeStruct((tile, tile), jnp.bfloat16),
+            jax.ShapeDtypeStruct((tile, tile), jnp.bfloat16),
         ),
         scratch_shapes=[
-            dma((Z_PARTS,)),
-            dma((Z_PARTS, y_parts)),
-            dma((Z_PARTS, y_parts)),
-            dma((cols,)),
+            pltpu.VMEM((tile, tile), jnp.float32),
+            pltpu.VMEM((tile, tile), jnp.float32),
+            dma((Z_PARTS, CHUNKS)),
+            dma((Z_PARTS, CHUNKS)),
+            dma((Z_PARTS, y_parts, CHUNKS)),
+            dma((Z_PARTS, y_parts, CHUNKS)),
+            dma((cols, CHUNKS)),
             dma((rows,)),
-            dma((tile // size,)),
-            dma((rows,)),
-            dma,
-            dma,
-            dma,
+            dma((spc,)),
+            dma((rows, spc, CHUNKS)),
+            dma((spc, CHUNKS)),
+            dma((spc, CHUNKS)),
             dma((cols,)),
             dma,
             dma((4,)),
         ],
-        compiler_params=pltpu.CompilerParams(collective_id=0, has_side_effects=True),
+        compiler_params=pltpu.CompilerParams(
+            collective_id=0, has_side_effects=True, vmem_limit_bytes=32 << 20
+        ),
         name="gather",
     )(landmarks, jit)
 
@@ -427,8 +542,7 @@
     cols = lax.axis_size("col")
     tile = jitter.shape[0]
     jit = jnp.broadcast_to(jitter.astype(jnp.float32)[None, :], (8, tile))
-    row_pts, col_pts, first_pts, first_jit = gather_call(rows, cols, landmarks, jit)
-    xh, xl = factor_call(first_pts, first_jit)
+    row_pts, col_pts, first_pts, first_jit, xh, xl = gather_call(rows, cols, landmarks, jit)
     return tuple(schur_call(cols // rows, row_pts, col_pts, first_pts, xh, xl, jit, first_jit))
 
 

time: 190 us -> 113 us (0.59)
  the two profiles are of different devices: /device:TPU:9 before, /device:TPU:3 now
where the time goes in v1:
time: 113 us; the launch traced here: 112 us
  Pallas kernels  107 us (95%)
  local copies, waits for them, and re-layouts  4.32 us (4%)
    pallas_call x1, Pallas kernels, gather_call(): pl.pallas_call(functools.partial(gather_kernel, rows, cols), in_specs=[hb...  79.2 us
    pallas_call x1, Pallas kernels, schur_call(): pl.pallas_call(functools.partial(schur_kernel, per_row), grid=(rowb // bm...  28.2 us
    unnamed x4, local copies, waits for them, and re-layouts  3.63 us

profile of v1, /device:TPU:3, one launch (start us, length us, event | category | flops | bytes accessed | tf_op | source)
XLA Modules:
  0.0 112.4 jit_solution(5652733784909374634)
XLA Ops:
  0.6 0.7 broadcast_in_dim.2.jit_ref
  1.3 0.0 copy-start.1
  1.3 1.0 copy-done.1
  2.3 79.2 %gather.1 = (bf16[4096,768]{1,0:T(8,128)(2,1)S(1)}, bf16[512,768]{1,0:T(8,128)(2,1)S(1)}, bf16[512,768]{1,0:T(8,128)(2,1)S(1)}, f32[8,512]{1,0:T(8,128)S(1)}, bf...) custom-call(bf16[256,768]{1,0:T(8,128)(2,1)S(1)} %copy-done.1, f32[8,512]{1,0:T(8,128)S(1)} %broadcast_in_dim.2.jit_ref), custom_call_target="tpu_custom_call" | custom-call | tf_op jit(solution)/shard_map/gather/pallas_call | solution.py:504
  81.6 0.0 copy-start
  81.6 2.6 %copy-done = bf16[4096,768]{1,0:T(8,128)(2,1)} copy-done((bf16[4096,768]{1,0:T(8,128)(2,1)}, bf16[4096,768]{1,0:T(8,128)(2,1)S(1)}, u32[]{:S(2)}) %copy-start) | copy-done | bytes 6291480
  84.2 28.2 %schur.1 = (f32[4096,512]{1,0:T(8,128)}, f32[4096,512]{1,0:T(8,128)}) custom-call(bf16[4096,768]{1,0:T(8,128)(2,1)} %copy-done, bf16[512,768]{1,0:T(8,128)(2,1)S(1)} %get-tuple-element.9.cols_ref, bf16[512,768]{1,0:T(8,128)(2,1)S(1)} %get-tuple-element.10.first_ref, bf16[512,512]{1,0:T(8,128)(2,1)S(1)} %get-tuple-element.11.xh_ref, ...), custom_call_target="tpu_custom_call" | custom-call | tf_op jit(solution)/shard_map/schur/pallas_call | solution.py:172
Async XLA Ops:
  1.3 1.0 copy-start.1
  81.6 2.6 %copy-start = (bf16[4096,768]{1,0:T(8,128)(2,1)}, bf16[4096,768]{1,0:T(8,128)(2,1)S(1)}, u32[]{:S(2)}) copy-start(bf16[4096,768]{1,0:T(8,128)(2,1)S(1)} %get-tuple-element.8.rows_ref) | copy-start | bytes 18874372

commit v2 on v1

--- a/solution.py
+++ b/solution.py
@@ -13,7 +13,8 @@
 STRIP = 8
 Z_PARTS = 4
 CORES = 2
-CHUNKS = 2
+CHUNKS = 4
+ORDER = ((1, 2, 3), (0, 2, 3), (3, 0, 1), (2, 0, 1))
 
 
 def dot_t(left, right, **kwargs):
@@ -166,7 +167,7 @@
 def schur_call(per_row, row_pts, col_pts, first_pts, xh, xl, jit, first_jit):
     rowb, width = row_pts.shape
     tile = col_pts.shape[0]
-    bm = min(512, rowb)
+    bm = min(1024, rowb)
     whole = lambda shape: pl.BlockSpec(shape, lambda i: (0, 0))
     out = jax.ShapeDtypeStruct((rowb, tile), jnp.float32)
     return pl.pallas_call(
@@ -301,41 +302,80 @@
         return remote(src, part(out_ref, i, h), send_k.at[z, y, h], recv.at[i, h],
                       me_row, sibling)
 
+    ahead = spc // CORES
+
+    def first_copy(src, d, s, h):
+        return remote(src, part(first_ref, s, h), send_f.at[d, s, h], recv_f.at[s, h], d, me)
+
+    def first_across(s, h):
+        return remote(part(first_ref, s, h), part(first_ref, s, h), send_fk.at[s, h],
+                      recv_f.at[s, h], me_row, sibling)
+
+    def first_rows(src, s, h):
+        @pl.when(me_row == 0)
+        def _():
+            for d in range(1, rows):
+                first_copy(src, d, s, h).start()
+
+    def first_aside(h):
+        for y in range(ahead):
+            s = index(0, y, core)
+
+            @pl.when(my_y != y)
+            def _():
+                landed(part(out_ref, s, h), recv.at[s, h])
+                first_rows(part(out_ref, s, h), s, h)
+                across(part(out_ref, s, h), 0, y, h).start()
+
+    def own_up(act, z):
+        for h in range(CHUNKS):
+            act(up(part(own_ref, 0, h), z, me, h))
+
     def walk(act, wait):
-        def spread(source, z, h, upward, downward):
+        def spread(here, z, h):
             i = index(z, my_y, core)
-            src = part(own_ref, 0, h) if source is own_ref else part(out_ref, i, h)
+            src = part(out_ref, i, h)
             if wait:
-                landed(part(out_ref, i, h), recv.at[i, h])
-            if upward:
-                @pl.when(my_z < Z_PARTS - 1)
+                landed(src, recv.at[i, h])
+            if z < here < Z_PARTS - 1:
+                act(up(src, z, i, h))
+            if z > here > 0:
+                act(down(src, z, i, h))
+            if wait and z == 0:
+                @pl.when(my_y < ahead)
                 def _():
-                    act(up(src, z, i, h))
-            if downward:
-                @pl.when(my_z > 0)
-                def _():
-                    act(down(src, z, i, h))
+                    first_rows(src, i, h)
             for d in range(1, y_parts):
                 act(aside(src, z, d, i, h))
             act(across(src, z, my_y, h))
 
-        for d in range(1, Z_PARTS):
-            for h in range(CHUNKS):
-                @pl.when(my_z >= d)
+        for here in range(Z_PARTS):
+            @pl.when(my_z == here)
+            def _():
+                if wait and here == 0:
+                    for h in range(CHUNKS):
+                        first_aside(h)
+                for z in ORDER[here]:
+                    for h in range(CHUNKS):
+                        spread(here, z, h)
+                    if z == 0 and here == 1:
+                        own_up(act, here)
+                    if z == 0 and wait:
+                        for h in range(CHUNKS):
+                            first_aside(h)
+
+    def own_copies(act, begins):
+        for here in range(Z_PARTS - 1):
+            if here != 1:
+                @pl.when(my_z == here)
                 def _():
-                    spread(out_ref, my_z - d, h, True, False)
-
-                @pl.when(my_z + d < Z_PARTS)
-                def _():
-                    spread(out_ref, my_z + d, h, False, True)
-
-    def own_copies(act):
+                    own_up(act, here)
         for h in range(CHUNKS):
             src = part(own_ref, 0, h)
-
-            @pl.when(my_z < Z_PARTS - 1)
-            def _():
-                act(up(src, my_z, me, h))
+            if begins:
+                @pl.when(me < spc)
+                def _():
+                    first_rows(src, me, h)
 
             @pl.when(my_z > 0)
             def _():
@@ -358,7 +398,7 @@
     def finish(copy):
         copy.wait_send()
 
-    own_copies(begin)
+    own_copies(begin, True)
     mine = pltpu.make_async_copy(own_ref, whole(out_ref, me), local.at[0])
     mine.start()
 
@@ -373,27 +413,6 @@
     walk(begin, True)
     mine.wait()
 
-    def first_copy(d, s, h):
-        return remote(part(out_ref, s, h), part(first_ref, s, h), send_f.at[d, s, h],
-                      recv_f.at[s, h], d, me)
-
-    def first_across(s, h):
-        return remote(part(first_ref, s, h), part(first_ref, s, h), send_fk.at[s, h],
-                      recv_f.at[s, h], me_row, sibling)
-
-    ahead = spc // CORES
-    for y in range(ahead):
-        s = index(0, y, core)
-        for h in range(CHUNKS):
-            @pl.when(my_y != y)
-            def _():
-                landed(part(out_ref, s, h), recv.at[s, h])
-                across(part(out_ref, s, h), 0, y, h).start()
-
-            @pl.when(me_row == 0)
-            def _():
-                for d in range(1, rows):
-                    first_copy(d, s, h).start()
     for y in range(ahead):
         s = index(0, y, core)
         for h in range(CHUNKS):
@@ -466,7 +485,7 @@
         for i in range(spc):
             landed(whole(col_ref, i), recv_x.at[i])
 
-    own_copies(finish)
+    own_copies(finish, False)
     walk(finish, False)
     for z in range(Z_PARTS):
         for d in range(1, y_parts):
@@ -481,7 +500,7 @@
             @pl.when(me_row == 0)
             def _():
                 for d in range(1, rows):
-                    finish(first_copy(d, s, h))
+                    finish(first_copy(part(out_ref, s, h), d, s, h))
 
             @pl.when(me_row != 0)
             def _():

time: 113 us -> 107 us (0.947)
  the two profiles are of different devices: /device:TPU:3 before, /device:TPU:5 now
where the time goes in v2:
time: 107 us
  Pallas kernels  102 us (95%)
  local copies, waits for them, and re-layouts  4.32 us (4%)
    pallas_call x1, Pallas kernels, gather_call(): pl.pallas_call(functools.partial(gather_kernel, rows, cols), in_specs=[hb...  74 us
    pallas_call x1, Pallas kernels, schur_call(): pl.pallas_call(functools.partial(schur_kernel, per_row), grid=(rowb // bm...  27.6 us
    unnamed x4, local copies, waits for them, and re-layouts  3.63 us

profile of v2, /device:TPU:5, one launch (start us, length us, event | category | flops | bytes accessed | tf_op | source)
XLA Modules:
  0.0 106.6 jit_solution(17586850759614518512)
XLA Ops:
  0.6 0.7 broadcast_in_dim.2.jit_ref
  1.3 0.0 copy-start.1
  1.3 1.0 copy-done.1
  2.3 74.0 %gather.1 = (bf16[4096,768]{1,0:T(8,128)(2,1)S(1)}, bf16[512,768]{1,0:T(8,128)(2,1)S(1)}, bf16[512,768]{1,0:T(8,128)(2,1)S(1)}, f32[8,512]{1,0:T(8,128)S(1)}, bf...) custom-call(bf16[256,768]{1,0:T(8,128)(2,1)S(1)} %copy-done.1, f32[8,512]{1,0:T(8,128)S(1)} %broadcast_in_dim.2.jit_ref), custom_call_target="tpu_custom_call" | custom-call | tf_op jit(solution)/shard_map/gather/pallas_call | solution.py:523
  76.3 0.0 copy-start
  76.4 2.6 %copy-done = bf16[4096,768]{1,0:T(8,128)(2,1)} copy-done((bf16[4096,768]{1,0:T(8,128)(2,1)}, bf16[4096,768]{1,0:T(8,128)(2,1)S(1)}, u32[]{:S(2)}) %copy-start) | copy-done | bytes 6291480
  79.0 27.6 %schur.1 = (f32[4096,512]{1,0:T(8,128)}, f32[4096,512]{1,0:T(8,128)}) custom-call(bf16[4096,768]{1,0:T(8,128)(2,1)} %copy-done, bf16[512,768]{1,0:T(8,128)(2,1)S(1)} %get-tuple-element.9.cols_ref, bf16[512,768]{1,0:T(8,128)(2,1)S(1)} %get-tuple-element.10.first_ref, bf16[512,512]{1,0:T(8,128)(2,1)S(1)} %get-tuple-element.11.xh_ref, ...), custom_call_target="tpu_custom_call" | custom-call | tf_op jit(solution)/shard_map/schur/pallas_call | solution.py:173
Async XLA Ops:
  1.3 1.0 copy-start.1
  76.3 2.6 %copy-start = (bf16[4096,768]{1,0:T(8,128)(2,1)}, bf16[4096,768]{1,0:T(8,128)(2,1)S(1)}, u32[]{:S(2)}) copy-start(bf16[4096,768]{1,0:T(8,128)(2,1)S(1)} %get-tuple-element.8.rows_ref) | copy-start | bytes 18874372
